TPU v7x, 32 devices: a whole 2x2x4 slice. The times are simulated.
32 devices in a mesh: group: 2 (over x), patch: 16 (over z, y, core).
Axes of the slice: x: 2, y: 2, z: 4, core: 2. Of those that a mesh axis runs over, the one named last changes fastest.
Arguments:
- queries: bfloat16 [40960, 256], P(('group', 'patch')), parts along dimension 0, may hold values from -38 to 38
- key_rows: bfloat16 [40960, 256], P(('group', 'patch')), parts along dimension 0, may hold values from -38 to 38
- value_rows: bfloat16 [40960, 256], P(('group', 'patch')), parts along dimension 0, may hold values from -6 to 6
- grad_out: bfloat16 [40960, 256], P(('group', 'patch')), parts along dimension 0, may hold values from -6 to 6
- window_blocks: int32 [320, 15], P('patch'), may hold values from -1 to 319, as said below
Outputs:
- grad_queries: float32 [40960, 256], P(('group', 'patch')), parts along dimension 0
- grad_keys: float32 [40960, 256], P(('group', 'patch')), parts along dimension 0
- grad_values: float32 [40960, 256], P(('group', 'patch')), parts along dimension 0
There are 2 independent parts, one for each index of `group`. A program takes and returns all parts, laid end to end along the dimension named above; an argument that names none is the same for every part. Nothing has to cross between parts.
Inputs may be any that keep to these rules, and one draw needn't show every extreme that they name: `window_blocks`: row b lists the key blocks of query block b, which lies in stripe b // 20 at block row b % 20. Its live entries are distinct and come first, the rest are -1. Each live entry is a block whose block row differs from the query's by at most one and whose stripe is within two of the query's around the longitude circle, or, for a query in the first or last block row, the block of the same block row in the stripe 16 // 2 away. Some query blocks have all 15 entries live.
All inputs are finite; a program needn't handle non-finite values.
Results may differ from a plain program's by a relative error of at most 0.011.
Values may be sent and summed in bfloat16 or wider, within the bound.
A program may use at most 128 MiB of HBM per device.

v0:
```python
import jax
import jax.numpy as jnp
from jax import lax
from jax.sharding import PartitionSpec as P

HEADS = 8


def shifted(block, axis, distance):
    devices = range(lax.axis_size(axis))
    route = [((i - distance) % len(devices), i) for i in devices]
    return lax.ppermute(block, axis, route)


def attend(query_blk, dout_blk, key_blk, value_blk, live_keys):
    row_count, features = query_blk.shape
    head_size = features // HEADS
    scaling = head_size ** (-0.5)
    q_heads = query_blk.reshape(row_count, HEADS, head_size)
    d_heads = dout_blk.reshape(row_count, HEADS, head_size)
    k_heads = key_blk.reshape(-1, HEADS, head_size)
    v_heads = value_blk.reshape(-1, HEADS, head_size)
    scores = (
        jnp.einsum("qhd,khd->hqk", q_heads, k_heads, preferred_element_type=jnp.float32) * scaling
    )
    scores = jnp.where(live_keys[None, None, :], scores, jnp.float32(-1e30))
    row_max = jnp.max(scores, axis=2, keepdims=True)
    exp_scores = jnp.exp(scores - row_max)
    weights = exp_scores / jnp.sum(exp_scores, axis=2, keepdims=True)
    low_weights = weights.astype(jnp.bfloat16)
    attn_out = jnp.einsum("hqk,khd->qhd", low_weights, v_heads, preferred_element_type=jnp.float32)
    row_dots = jnp.sum(d_heads.astype(jnp.float32) * attn_out, axis=2)
    grad_weights = jnp.einsum("qhd,khd->hqk", d_heads, v_heads, preferred_element_type=jnp.float32)
    grad_scores = (weights * (grad_weights - jnp.transpose(row_dots)[:, :, None])).astype(
        jnp.bfloat16
    )
    grad_q = (
        jnp.einsum("hqk,khd->qhd", grad_scores, k_heads, preferred_element_type=jnp.float32)
        * scaling
    )
    grad_k = (
        jnp.einsum("hqk,qhd->khd", grad_scores, q_heads, preferred_element_type=jnp.float32)
        * scaling
    )
    grad_v = jnp.einsum("hqk,qhd->khd", low_weights, d_heads, preferred_element_type=jnp.float32)
    return (
        grad_q.reshape(row_count, features),
        grad_k.reshape(-1, features),
        grad_v.reshape(-1, features),
    )


def local(queries, key_rows, value_rows, grad_out, window_blocks):
    token_count, features = queries.shape
    band_count = window_blocks.shape[0]
    block_len = token_count // band_count
    stripes = lax.axis_size("patch")
    half_turn = stripes // 2
    stripe = lax.axis_index("patch")
    stacked = jnp.stack([key_rows, value_rows]).reshape(2, band_count, block_len, features)
    fetched = {0: stacked}
    for distance in (-2, -1, 1, 2):
        fetched[distance] = shifted(stacked, "patch", -distance)
    pole_rows = jnp.concatenate([stacked[:, :1], stacked[:, band_count - 1 :]], axis=1)
    pole_keys = shifted(pole_rows, "patch", half_turn)
    window = jnp.concatenate(
        [fetched[-2], fetched[-1], fetched[0], fetched[1], fetched[2], pole_keys], axis=1
    )
    live = window_blocks >= 0
    safe_ids = jnp.where(live, window_blocks, 0)
    source = safe_ids // band_count
    band_of = safe_ids % band_count
    delta = (source - stripe) % stripes
    nearby = jnp.where(delta <= 2, delta, delta - stripes) + 2
    position = jnp.where(
        delta == half_turn,
        5 * band_count + jnp.where(band_of == 0, 0, 1),
        nearby * band_count + band_of,
    )
    position = jnp.where(live, position, 2 * band_count)
    query_blocks = queries.reshape(band_count, block_len, features)
    dout_blocks = grad_out.reshape(band_count, block_len, features)

    def advance(band, carry):
        totals, grad_rows = carry
        picks = position[band]
        token_live = jnp.repeat(live[band], block_len)
        chosen = jnp.take(window, picks, axis=1).reshape(2, -1, features)
        grad_q, grad_k, grad_v = attend(
            query_blocks[band], dout_blocks[band], chosen[0], chosen[1], token_live
        )
        update = jnp.stack([grad_k, grad_v]).reshape(2, -1, block_len, features)
        totals = totals.at[:, picks].add(update)
        grad_rows = grad_rows.at[band].set(grad_q)
        return (totals, grad_rows)

    zero_totals = jnp.zeros((2, 5 * band_count + 2, block_len, features), jnp.float32)
    zero_rows = jnp.zeros((band_count, block_len, features), jnp.float32)
    totals, grad_rows = lax.fori_loop(0, band_count, advance, (zero_totals, zero_rows))

    def partial_of(distance):
        return totals[:, (distance + 2) * band_count : (distance + 3) * band_count]

    owned = partial_of(0)
    for distance in (-2, -1, 1, 2):
        owned = owned + shifted(partial_of(distance), "patch", distance)
    pole_back = shifted(
        totals[:, 5 * band_count :].astype(jnp.bfloat16), "patch", half_turn
    ).astype(jnp.float32)
    owned = owned.at[:, 0].add(pole_back[:, 0])
    owned = owned.at[:, band_count - 1].add(pole_back[:, 1])
    grad_keys = owned[0].reshape(token_count, features)
    grad_values = owned[1].reshape(token_count, features)
    return (grad_rows.reshape(token_count, features), grad_keys, grad_values)


def solution(mesh):
    return jax.shard_map(
        local,
        mesh=mesh,
        in_specs=(
            P(("group", "patch"), None),
            P(("group", "patch"), None),
            P(("group", "patch"), None),
            P(("group", "patch"), None),
            P("patch", None),
        ),
        out_specs=(
            P(("group", "patch"), None),
            P(("group", "patch"), None),
            P(("group", "patch"), None),
        ),
        check_vma=False,
    )
```

profile of v0, /device:TPU:1, one launch (start us, length us, event | category | flops | bytes accessed | tf_op | source)
XLA Modules:
  0.0 886.7 jit_solution(13575167416303217786)
XLA Ops:
  10.1 63.8 %collective-permute-done = bf16[2,20,64,256]{3,2,1,0:T(8,128)(2,1)} collective-permute-done((bf16[2,20,64,256]{3,2,1,0:T(8,128)(2,1)S(1)}, bf16[2,20,64,256]{3,2,1,0:T(8,128)(2,1)}, u32[]{:S(2)}, u32[]{:S(2)}) %collective-permute-start) | collective-permute-done | bytes 1310752 | tf_op jit(solution)/shard_map/ppermute | solution.py:12
  76.4 12.7 %collective-permute-done.1 = bf16[2,20,64,256]{3,2,1,0:T(8,128)(2,1)} collective-permute-done((bf16[2,20,64,256]{3,2,1,0:T(8,128)(2,1)S(1)}, bf16[2,20,64,256]{3,2,1,0:T(8,128)(2,1)}, u32[]{:S(2)}, u32[]{:S(2)}) %collective-permute-start.1) | collective-permute-done | bytes 1310752 | tf_op jit(solution)/shard_map/ppermute | solution.py:12
  99.7 6.5 broadcast_in_dim.83
  106.2 599.7 %while.18 = (s32[]{:T(128)}, f32[2,102,64,256]{3,2,1,0:T(8,128)}, f32[20,64,256]{2,1,0:T(8,128)}, s32[20,15]{1,0:T(8,128)S(1)}, bf16[20,64,256]{2,1,0:T(8,128)(2...) while((s32[]{:T(128)}, f32[2,102,64,256]{3,2,1,0:T(8,128)}, ...), condition=%wide.region_6.7_spmd, body=%wide.region_0.6_spmd.sunk | while | flops 195462736 | bytes 68078504 | solution.py:99
  131.7 4.3 scatter_fusion
  161.6 4.4 scatter_fusion
  191.5 4.5 scatter_fusion
  221.6 4.6 scatter_fusion
  251.8 4.3 scatter_fusion
  311.5 4.5 scatter_fusion
  341.6 4.5 scatter_fusion
  461.2 4.5 scatter_fusion
  491.3 4.5 scatter_fusion
  521.4 4.5 scatter_fusion
  551.4 4.3 scatter_fusion
  581.3 4.6 scatter_fusion
  611.4 4.5 scatter_fusion
  641.5 4.4 scatter_fusion
  671.4 4.5 scatter_fusion
  701.5 4.4 scatter_fusion
  705.9 4.9 fusion.28
  719.5 51.0 %collective-permute-done.9 = bf16[2,2,64,256]{3,2,1,0:T(8,128)(2,1)S(1)} collective-permute-done((bf16[2,2,64,256]{3,2,1,0:T(8,128)(2,1)S(1)}, bf16[2,2,64,256]{3,2,1,0:T(8,128)(2,1)S(1)}, u32[]{:S(2)}, u32[]{:S(2)}) %collective-permute-start.9) | collective-permute-done | bytes 131104 | tf_op jit(solution)/shard_map/ppermute | solution.py:12
  770.6 82.0 %collective-permute-done.5 = f32[2,20,64,256]{3,2,1,0:T(8,128)S(1)} collective-permute-done((f32[2,20,64,256]{3,2,1,0:T(8,128)S(1)}, f32[2,20,64,256]{3,2,1,0:T(8,128)S(1)}, u32[]{:S(2)}, u32[]{:S(2)}) %collective-permute-start.5) | collective-permute-done | bytes 2621472 | tf_op jit(solution)/shard_map/ppermute | solution.py:12
  852.9 28.2 %collective-permute-done.7 = f32[2,20,64,256]{3,2,1,0:T(8,128)S(1)} collective-permute-done((f32[2,20,64,256]{3,2,1,0:T(8,128)S(1)}, f32[2,20,64,256]{3,2,1,0:T(8,128)S(1)}, u32[]{:S(2)}, u32[]{:S(2)}) %collective-permute-start.7) | collective-permute-done | bytes 2621472 | tf_op jit(solution)/shard_map/ppermute | solution.py:12
  (866 shorter events, 562.3 us)
Async XLA Ops:
  0.6 8.7 copy-start.3
  0.6 8.7 copy-start.4
  0.7 9.3 %copy-start.6 = (s32[20,15]{0,1:T(8,128)S(1)}, s32[20,15]{0,1:T(8,128)}, u32[]{:S(2)}) copy-start(s32[20,15]{0,1:T(8,128)} %param.17) | copy-start | bytes 3604
  2.2 71.7 %collective-permute-start = (bf16[2,20,64,256]{3,2,1,0:T(8,128)(2,1)S(1)}, bf16[2,20,64,256]{3,2,1,0:T(8,128)(2,1)}, u32[]{:S(2)}, u32[]{:S(2)}) collective-permute-start(bf16[2,20,64,256]{3,2,1,0:T(8,128)(2,1)S(1)} %pad_maximum_fusion), channel_id=1, source_target_pairs={{14,0},{15,1},{0,2},{1,3},{2,4},{3,5},{4,6},{5,7},{6,8},{7,9},{8,1... | collective-permute-start | bytes 3932168 | tf_op jit(solution)/shard_map/ppermute | solution.py:12
  4.3 84.8 %collective-permute-start.1 = (bf16[2,20,64,256]{3,2,1,0:T(8,128)(2,1)S(1)}, bf16[2,20,64,256]{3,2,1,0:T(8,128)(2,1)}, u32[]{:S(2)}, u32[]{:S(2)}) collective-permute-start(bf16[2,20,64,256]{3,2,1,0:T(8,128)(2,1)S(1)} %pad_maximum_fusion), channel_id=1, source_target_pairs={{15,0},{0,1},{1,2},{2,3},{3,4},{4,5},{5,6},{6,7},{7,8},{8,9},{9,10... | collective-permute-start | bytes 3932168 | tf_op jit(solution)/shard_map/ppermute | solution.py:12
  6.4 86.4 %collective-permute-start.2 = (bf16[2,20,64,256]{3,2,1,0:T(8,128)(2,1)S(1)}, bf16[2,20,64,256]{3,2,1,0:T(8,128)(2,1)}, u32[]{:S(2)}, u32[]{:S(2)}) collective-permute-start(bf16[2,20,64,256]{3,2,1,0:T(8,128)(2,1)S(1)} %pad_maximum_fusion), channel_id=1, source_target_pairs={{1,0},{2,1},{3,2},{4,3},{5,4},{6,5},{7,6},{8,7},{9,8},{10,9},{11,1... | collective-permute-start | bytes 3932168 | tf_op jit(solution)/shard_map/ppermute | solution.py:12
  6.4 88.9 %collective-permute-start.3 = (bf16[2,20,64,256]{3,2,1,0:T(8,128)(2,1)S(1)}, bf16[2,20,64,256]{3,2,1,0:T(8,128)(2,1)}, u32[]{:S(2)}, u32[]{:S(2)}) collective-permute-start(bf16[2,20,64,256]{3,2,1,0:T(8,128)(2,1)S(1)} %pad_maximum_fusion), channel_id=1, source_target_pairs={{2,0},{3,1},{4,2},{5,3},{6,4},{7,5},{8,6},{9,7},{10,8},{11,9},{12,... | collective-permute-start | bytes 3932168 | tf_op jit(solution)/shard_map/ppermute | solution.py:12
  9.4 88.4 %collective-permute-start.4 = (bf16[2,2,64,256]{3,2,1,0:T(8,128)(2,1)S(1)}, bf16[2,2,64,256]{3,2,1,0:T(8,128)(2,1)S(1)}, u32[]{:S(2)}, u32[]{:S(2)}) collective-permute-start(bf16[2,2,64,256]{3,2,1,0:T(8,128)(2,1)S(1)} %pad_maximum_fusion.1), channel_id=1, source_target_pairs={{8,0},{9,1},{10,2},{11,3},{12,4},{13,5},{14,6},{15,7},{0,8},{1,9},... | collective-permute-start | bytes 393224 | tf_op jit(solution)/shard_map/ppermute | solution.py:12
  99.7 6.5 copy-start.5
  127.7 1.9 copy-start
  157.6 1.9 copy-start
  187.5 1.9 copy-start
  217.6 1.9 copy-start
  277.6 1.9 copy-start
  307.5 1.9 copy-start
  337.5 1.9 copy-start
  367.6 1.9 copy-start
  397.5 1.9 copy-start
  427.3 1.9 copy-start
  710.8 141.7 %collective-permute-start.5 = (f32[2,20,64,256]{3,2,1,0:T(8,128)S(1)}, f32[2,20,64,256]{3,2,1,0:T(8,128)S(1)}, u32[]{:S(2)}, u32[]{:S(2)}) collective-permute-start(f32[2,20,64,256]{3,2,1,0:T(8,128)S(1)} %get-tuple-element.237), channel_id=1, source_target_pairs={{2,0},{3,1},{4,2},{5,3},{6,4},{7,5},{8,6},{9,7},{10,8},{11,9},{12,... | collective-permute-start | bytes 7864328 | tf_op jit(solution)/shard_map/ppermute | solution.py:12
  710.9 142.0 %collective-permute-start.8 = (f32[2,20,64,256]{3,2,1,0:T(8,128)S(1)}, f32[2,20,64,256]{3,2,1,0:T(8,128)S(1)}, u32[]{:S(2)}, u32[]{:S(2)}) collective-permute-start(f32[2,20,64,256]{3,2,1,0:T(8,128)S(1)} %get-tuple-element.238), channel_id=1, source_target_pairs={{14,0},{15,1},{0,2},{1,3},{2,4},{3,5},{4,6},{5,7},{6,8},{7,9},{8,1... | collective-permute-start | bytes 7864328 | tf_op jit(solution)/shard_map/ppermute | solution.py:12
  712.3 168.8 %collective-permute-start.7 = (f32[2,20,64,256]{3,2,1,0:T(8,128)S(1)}, f32[2,20,64,256]{3,2,1,0:T(8,128)S(1)}, u32[]{:S(2)}, u32[]{:S(2)}) collective-permute-start(f32[2,20,64,256]{3,2,1,0:T(8,128)S(1)} %get-tuple-element.239), channel_id=1, source_target_pairs={{15,0},{0,1},{1,2},{2,3},{3,4},{4,5},{5,6},{6,7},{7,8},{8,9},{9,10... | collective-permute-start | bytes 7864328 | tf_op jit(solution)/shard_map/ppermute | solution.py:12
  716.4 165.4 %collective-permute-start.6 = (f32[2,20,64,256]{3,2,1,0:T(8,128)S(1)}, f32[2,20,64,256]{3,2,1,0:T(8,128)S(1)}, u32[]{:S(2)}, u32[]{:S(2)}) collective-permute-start(f32[2,20,64,256]{3,2,1,0:T(8,128)S(1)} %get-tuple-element.240), channel_id=1, source_target_pairs={{1,0},{2,1},{3,2},{4,3},{5,4},{6,5},{7,6},{8,7},{9,8},{10,9},{11,1... | collective-permute-start | bytes 7864328 | tf_op jit(solution)/shard_map/ppermute | solution.py:12
  717.9 52.6 %collective-permute-start.9 = (bf16[2,2,64,256]{3,2,1,0:T(8,128)(2,1)S(1)}, bf16[2,2,64,256]{3,2,1,0:T(8,128)(2,1)S(1)}, u32[]{:S(2)}, u32[]{:S(2)}) collective-permute-start(bf16[2,2,64,256]{3,2,1,0:T(8,128)(2,1)S(1)} %slice.193), channel_id=1, source_target_pairs={{8,0},{9,1},{10,2},{11,3},{12,4},{13,5},{14,6},{15,7},{0,8},{1,9},... | collective-permute-start | bytes 393224 | tf_op jit(solution)/shard_map/ppermute | solution.py:12
  (50 other events, 78.5 us)
where the time goes:
time: 893 us; the launch traced here: 887 us
  local copies, waits for them, and re-layouts  395 us (44%)
  waiting for transfers between devices  239 us (27%)
  other arithmetic  158 us (18%)
  matrix products  75.6 us (8%)
  starting transfers between devices  15.5 us (2%)
    ppermute x10, waiting for transfers between devices, shifted(): return lax.ppermute(block, axis, route)  239 us
    another operation x100, local copies, waits for them, and re-layouts, advance(): update = jnp.stack([grad_k, grad_v]).reshape(2, -1, block_len, features)  126 us
    scatter-add x20, other arithmetic, advance(): totals = totals.at[:, picks].add(update)  88.6 us
    gather x20, local copies, waits for them, and re-layouts, advance(): chosen = jnp.take(window, picks, axis=1).reshape(2, -1, features)  70.2 us
    while x120, local copies, waits for them, and re-layouts  47.2 us
    another operation x40, other arithmetic  27.6 us
    another operation x20, other arithmetic, advance(): update = jnp.stack([grad_k, grad_v]).reshape(2, -1, block_len, features)  26.6 us
    dot_general x20, matrix products, attend(): jnp.einsum('hqk,qhd->khd', grad_scores, q_heads, preferred_element_type=j...  25.2 us
  transfers between devices with their start and end apart: 10, of which 7 were waited for; matrix products, arithmetic and copies ran while one was open for 1% of the time, Pallas kernels for 0%

commit v1 on v0

v1 whole, which is shorter than its diff:
```python
import functools
import math

import jax
import jax.numpy as jnp
from jax import lax
from jax.experimental import pallas as pl
from jax.experimental.pallas import tpu as pltpu
from jax.sharding import PartitionSpec as P

HEADS = 8
REACH = 2
SLOTS = 2 * REACH + 1


def shifted(block, distance):
    n = lax.axis_size("patch")
    return lax.ppermute(block, "patch", [((i - distance) % n, i) for i in range(n)])


def swapped(block):
    n = lax.axis_size("patch")
    return lax.ppermute(block, "patch", [(i, i ^ 1) for i in range(n)])


def block_diagonal(rows):
    head = lax.broadcasted_iota(jnp.int32, rows.shape, 1) // (rows.shape[1] // HEADS)
    zero = jnp.zeros_like(rows)
    return jnp.concatenate([jnp.where(head == h, rows, zero) for h in range(HEADS)], axis=0)


def dot(a, b, dim_a, dim_b):
    return lax.dot_general(
        a, b, (((dim_a,), (dim_b,)), ((), ())), preferred_element_type=jnp.float32
    )


def attend_band(band, block, bias, queries, grad_out, kv, totals, grad_queries, probs, grads):
    features = queries.shape[1]
    scale = (features // HEADS) ** (-0.5)
    rows = pl.ds(pl.multiple_of(band * block, block), block)
    window = pl.ds(pl.multiple_of(band * block, block), 3 * block)
    q = block_diagonal(queries[rows, :])
    d = block_diagonal(grad_out[rows, :])
    top = None
    for slot in range(SLOTS):
        raw = dot(kv[slot, 0, window, :], q, 1, 1) * jnp.float32(scale * math.log2(math.e))
        for part in range(3):
            piece = raw[part * block : (part + 1) * block] + bias[band, slot * 3 + part]
            probs[(slot * 3 + part) * block : (slot * 3 + part + 1) * block, :] = piece
            peak = jnp.max(piece, axis=0, keepdims=True)
            top = peak if top is None else jnp.maximum(top, peak)
    norm = jnp.zeros_like(top)
    row_dot = jnp.zeros_like(top)
    for slot in range(SLOTS):
        span = slice(slot * 3 * block, (slot + 1) * 3 * block)
        p = jnp.exp2(probs[span, :] - top)
        g = dot(kv[slot, 1, window, :], d, 1, 1)
        norm += jnp.sum(p, axis=0, keepdims=True)
        row_dot += jnp.sum(p * g, axis=0, keepdims=True)
        probs[span, :] = p
        grads[span, :] = g
    inverse = 1.0 / norm
    row_dot = row_dot * inverse
    grad_q = None
    for slot in range(SLOTS):
        span = slice(slot * 3 * block, (slot + 1) * 3 * block)
        w = probs[span, :] * inverse
        g = (w * (grads[span, :] - row_dot)).astype(jnp.bfloat16)
        totals[slot, 1, window, :] += dot(w.astype(jnp.bfloat16), d, 1, 0)
        totals[slot, 0, window, :] += dot(g, q, 1, 0)
        term = dot(kv[slot, 0, window, :], g, 0, 0)
        grad_q = term if grad_q is None else grad_q + term
    head_row = lax.broadcasted_iota(jnp.int32, grad_q.shape, 0) // (features // HEADS)
    head_col = lax.broadcasted_iota(jnp.int32, grad_q.shape, 1) // block
    grad_q = jnp.where(head_row == head_col, grad_q, 0.0)
    pair = 2 * block
    folded = grad_q[:, :pair]
    for at in range(pair, HEADS * block, pair):
        folded = folded + grad_q[:, at : at + pair]
    folded = folded.T
    grad_queries[rows, :] = (folded[:block] + folded[block:]) * scale


def kernel(block, bias, queries, grad_out, kv, grad_queries, totals, probs, grads):
    totals[...] = jnp.zeros_like(totals)

    def step(band, carry):
        attend_band(band, block, bias, queries, grad_out, kv, totals, grad_queries, probs, grads)
        return carry

    lax.fori_loop(0, queries.shape[0] // block, step, 0)


def bias_of(window_blocks):
    bands = window_blocks.shape[0]
    stripes = lax.axis_size("patch")
    stripe = lax.axis_index("patch")
    band = jnp.arange(bands, dtype=jnp.int32)[:, None, None]
    slot = jnp.arange(SLOTS, dtype=jnp.int32)[None, :, None]
    row = band + jnp.arange(-1, 2, dtype=jnp.int32)[None, None, :]
    inside = (row >= 0) & (row < bands)
    regular = (stripe + slot - REACH) % stripes * bands + row
    across = jnp.where(slot == REACH, (stripe + stripes // 2) % stripes * bands + band, -2)
    wanted = jnp.where(inside, regular, across)
    live = jnp.any(wanted[..., None] == window_blocks[:, None, None, :], axis=-1)
    return jnp.where(live, 0.0, -1e30).astype(jnp.float32).reshape(bands, SLOTS * 3)


def local(queries, key_rows, value_rows, grad_out, window_blocks):
    tokens, features = queries.shape
    bands = window_blocks.shape[0]
    block = tokens // bands
    half_turn = lax.axis_size("patch") // 2
    even = lax.axis_index("patch") % 2 == 0
    bias = bias_of(window_blocks)
    own = jnp.stack([key_rows, value_rows])
    after = shifted(own, -2)
    before = shifted(own, 2)
    near = swapped(own)
    far = swapped(jnp.where(even, after, before))
    poles = shifted(jnp.concatenate([own[:, :block], own[:, tokens - block :]], axis=1), half_turn)
    pad = lambda x: jnp.pad(x, ((0, 0), (block, block), (0, 0)))
    kv = jnp.stack(
        [
            pad(before),
            pad(jnp.where(even, far, near)),
            jnp.concatenate([poles[:, :block], own, poles[:, block:]], axis=1),
            pad(jnp.where(even, near, far)),
            pad(after),
        ]
    )
    vmem = pl.BlockSpec(memory_space=pltpu.VMEM)
    grad_rows, totals = pl.pallas_call(
        functools.partial(kernel, block),
        out_shape=(
            jax.ShapeDtypeStruct((tokens, features), jnp.float32),
            jax.ShapeDtypeStruct(kv.shape, jnp.float32),
        ),
        in_specs=[pl.BlockSpec(memory_space=pltpu.SMEM), vmem, vmem, vmem],
        out_specs=(vmem, vmem),
        scratch_shapes=[
            pltpu.VMEM((SLOTS * 3 * block, HEADS * block), jnp.float32),
            pltpu.VMEM((SLOTS * 3 * block, HEADS * block), jnp.float32),
        ],
        compiler_params=pltpu.CompilerParams(vmem_limit_bytes=56 * 2**20),
    )(bias, queries, grad_out, kv)
    scale = jnp.array([(features // HEADS) ** (-0.5), 1.0], jnp.float32)[:, None, None]
    totals = totals * scale
    inner = totals[:, :, block : block + tokens]
    low = inner.astype(jnp.bfloat16)
    far = swapped(jnp.where(even, low[1], low[3])).astype(jnp.float32)
    zero = jnp.zeros_like(far)
    to_after = (inner[4] + jnp.where(even, far, zero)).astype(jnp.bfloat16)
    to_before = (inner[0] + jnp.where(even, zero, far)).astype(jnp.bfloat16)
    near = swapped(jnp.where(even, low[3], low[1])).astype(jnp.float32)
    pole_parts = jnp.concatenate([totals[2, :, :block], totals[2, :, block + tokens :]], axis=1)
    pole_back = shifted(pole_parts.astype(jnp.bfloat16), half_turn).astype(jnp.float32)
    owned = (
        inner[2]
        + near
        + shifted(to_after, 2).astype(jnp.float32)
        + shifted(to_before, -2).astype(jnp.float32)
    )
    owned = owned.at[:, :block].add(pole_back[:, :block])
    owned = owned.at[:, tokens - block :].add(pole_back[:, block:])
    return grad_rows, owned[0], owned[1]


def solution(mesh):
    spec = P(("group", "patch"), None)
    return jax.shard_map(
        local,
        mesh=mesh,
        in_specs=(spec, spec, spec, spec, P("patch", None)),
        out_specs=(spec, spec, spec),
        check_vma=False,
    )
```

time: 893 us -> 212 us (0.24)
  the two profiles are of different devices: /device:TPU:1 before, /device:TPU:0 now
where the time goes in v1:
time: 212 us; the launch traced here: 211 us
  waiting for transfers between devices  113 us (53%)
  Pallas kernels  60.9 us (29%)
  other arithmetic  14 us (7%)
  starting transfers between devices  13 us (6%)
  local copies, waits for them, and re-layouts  9.17 us (4%)
    ppermute x6, waiting for transfers between devices, shifted(): lax.ppermute(block, 'patch', [((i - distance) % n, i) for i in range(n)])  110 us
    pallas_call x1, Pallas kernels, local(): pl.pallas_call(functools.partial(kernel, block), out_shape=(jax.ShapeDtyp...  60.9 us
    ppermute x6, starting transfers between devices, shifted(): lax.ppermute(block, 'patch', [((i - distance) % n, i) for i in range(n)])  11.1 us
    unnamed x19, local copies, waits for them, and re-layouts  6.7 us
    another operation x1, other arithmetic  6.4 us
  transfers between devices with their start and end apart: 10, of which 7 were waited for; matrix products, arithmetic and copies ran while one was open for 2% of the time, Pallas kernels for 0%

profile of v1, /device:TPU:0, one launch (start us, length us, event | category | flops | bytes accessed | tf_op | source)
XLA Modules:
  0.0 211.4 jit_solution(13393392310785225964)
XLA Ops:
  0.7 2.6 %pad_maximum_fusion = bf16[2,1280,256]{2,1,0:T(8,128)(2,1)} fusion(bf16[1,1280,256]{2,1,0:T(8,128)(2,1)} %bitcast.44, bf16[1,1280,256]{2,1,0:T(8,128)(2,1)} %bitcast.47), kind=kLoop, calls=%fused_computation.15 | loop fusion | flops 655360 | bytes 2621440 | tf_op jit(solution)/shard_map/stack | solution.py:117
  3.2 6.0 %collective-permute-start.1 = (bf16[2,1280,256]{2,1,0:T(8,128)(2,1)}, bf16[2,1280,256]{2,1,0:T(8,128)(2,1)S(1)}, u32[]{:S(2)}, u32[]{:S(2)}) collective-permute-start(bf16[2,1280,256]{2,1,0:T(8,128)(2,1)} %pad_maximum_fusion), channel_id=1, source_target_pairs={{2,0},{3,1},{4,2},{5,3},{6,4},{7,5},{8,6},{9,7},{10,8},{11,9},{12,... | collective-permute-start | bytes 3932168 | tf_op jit(solution)/shard_map/ppermute | solution.py:18
  9.6 53.7 %collective-permute-done.1 = bf16[2,1280,256]{2,1,0:T(8,128)(2,1)S(1)} collective-permute-done((bf16[2,1280,256]{2,1,0:T(8,128)(2,1)}, bf16[2,1280,256]{2,1,0:T(8,128)(2,1)S(1)}, u32[]{:S(2)}, u32[]{:S(2)}) %collective-permute-start.1) | collective-permute-done | bytes 1310752 | tf_op jit(solution)/shard_map/ppermute | solution.py:18
  63.5 1.2 broadcast_select_fusion.2
  64.7 1.3 collective-permute-start.2
  66.3 0.7 copy.12.bias
  67.0 1.4 bitcast_dynamic-update-slice_fusion.3
  68.4 0.6 collective-permute-done.2
  69.1 1.9 broadcast_select_fusion
  71.1 1.0 copy-done.3
  72.2 1.2 copy-done.5
  73.6 2.9 %copy-done = bf16[5,2,1408,256]{3,2,1,0:T(8,128)(2,1)} copy-done((bf16[5,2,1408,256]{3,2,1,0:T(8,128)(2,1)}, bf16[5,2,1408,256]{3,2,1,0:T(8,128)(2,1)S(1)}, u32[]{:S(2)}) %copy-start) | copy-done | bytes 7208984
  76.4 60.9 %shard_map.85 = (f32[1280,256]{1,0:T(8,128)}, f32[5,2,1408,256]{3,2,1,0:T(8,128)}) custom-call(f32[20,15]{1,0:T(8,128)} %copy.12.bias, bf16[1280,256]{1,0:T(8,128)(2,1)} %queries.1, bf16[1280,256]{1,0:T(8,128)(2,1)} %grad_out.1, bf16[5,2,1408,256]{3,2,1,0:T(8,128)(2,1)} %copy-done), custom_call_target="tpu_custom_call" | custom-call | tf_op jit(solution)/shard_map/pallas_call | solution.py:134
  137.4 6.4 %fusion.14 = (bf16[5,2,1408,256]{3,2,1,0:T(8,128)(2,1)S(1)}, f32[5,2,1408,256]{3,2,1,0:T(8,128)S(1)}) fusion(f32[5,2,1408,256]{3,2,1,0:T(8,128)} %get-tuple-element.30, f32[2]{0:T(128)S(1)} %copy-done.7), kind=kLoop, calls=%fused_computation.55 | loop fusion | flops 7208960 | bytes 36044808 | tf_op jit(solution)/shard_map/convert.6
  144.0 0.4 collective-permute-start.6
  144.6 2.5 %collective-permute-done.6 = bf16[2,1280,256]{2,1,0:T(8,128)(2,1)S(1)} collective-permute-done((bf16[2,1280,256]{2,1,0:T(8,128)(2,1)S(1)}, bf16[2,1280,256]{2,1,0:T(8,128)(2,1)S(1)}, u32[]{:S(2)}, u32[]{:S(2)}) %collective-permute-start.6) | collective-permute-done | bytes 1310752 | tf_op jit(solution)/shard_map/ppermute | solution.py:23
  147.1 0.7 fusion.1
  147.8 2.5 %collective-permute-start.7 = (bf16[2,1280,256]{2,1,0:T(8,128)(2,1)S(1)}, bf16[2,1280,256]{2,1,0:T(8,128)(2,1)S(1)}, u32[]{:S(2)}, u32[]{:S(2)}) collective-permute-start(bf16[2,1280,256]{2,1,0:T(8,128)(2,1)S(1)} %get-tuple-element.31), channel_id=1, source_target_pairs={{14,0},{15,1},{0,2},{1,3},{2,4},{3,5},{4,6},{5,7},{6,8},{7,9},{8,1... | collective-permute-start | bytes 3932168 | tf_op jit(solution)/shard_map/ppermute | solution.py:18
  150.3 2.2 %collective-permute-start.8 = (bf16[2,1280,256]{2,1,0:T(8,128)(2,1)S(1)}, bf16[2,1280,256]{2,1,0:T(8,128)(2,1)S(1)}, u32[]{:S(2)}, u32[]{:S(2)}) collective-permute-start(bf16[2,1280,256]{2,1,0:T(8,128)(2,1)S(1)} %get-tuple-element.32), channel_id=1, source_target_pairs={{2,0},{3,1},{4,2},{5,3},{6,4},{7,5},{8,6},{9,7},{10,8},{11,9},{12,... | collective-permute-start | bytes 3932168 | tf_op jit(solution)/shard_map/ppermute | solution.py:18
  152.8 34.3 %collective-permute-done.9 = bf16[2,128,256]{2,1,0:T(8,128)(2,1)S(1)} collective-permute-done((bf16[2,128,256]{2,1,0:T(8,128)(2,1)S(1)}, bf16[2,128,256]{2,1,0:T(8,128)(2,1)S(1)}, u32[]{:S(2)}, u32[]{:S(2)}) %collective-permute-start.9) | collective-permute-done | bytes 131104 | tf_op jit(solution)/shard_map/ppermute | solution.py:18
  187.1 19.8 %collective-permute-done.7 = bf16[2,1280,256]{2,1,0:T(8,128)(2,1)S(1)} collective-permute-done((bf16[2,1280,256]{2,1,0:T(8,128)(2,1)S(1)}, bf16[2,1280,256]{2,1,0:T(8,128)(2,1)S(1)}, u32[]{:S(2)}, u32[]{:S(2)}) %collective-permute-start.7) | collective-permute-done | bytes 1310752 | tf_op jit(solution)/shard_map/ppermute | solution.py:18
  206.9 2.2 %collective-permute-done.8 = bf16[2,1280,256]{2,1,0:T(8,128)(2,1)S(1)} collective-permute-done((bf16[2,1280,256]{2,1,0:T(8,128)(2,1)S(1)}, bf16[2,1280,256]{2,1,0:T(8,128)(2,1)S(1)}, u32[]{:S(2)}, u32[]{:S(2)}) %collective-permute-start.8) | collective-permute-done | bytes 1310752 | tf_op jit(solution)/shard_map/ppermute | solution.py:18
  209.1 0.5 fusion.6
  209.7 1.7 slice_bitcast_fusion.3
  (46 shorter events, 1.9 us)
Async XLA Ops:
  0.6 8.6 %copy-start.1 = (bf16[1280,256]{1,0:T(8,128)(2,1)S(1)}, bf16[1280,256]{1,0:T(8,128)(2,1)}, u32[]{:S(2)}) copy-start(bf16[1280,256]{1,0:T(8,128)(2,1)} %param.12) | copy-start | bytes 1966084
  0.6 8.6 %copy-start.2 = (bf16[1280,256]{1,0:T(8,128)(2,1)S(1)}, bf16[1280,256]{1,0:T(8,128)(2,1)}, u32[]{:S(2)}) copy-start(bf16[1280,256]{1,0:T(8,128)(2,1)} %param.11) | copy-start | bytes 1966084
  3.2 60.0 %collective-permute-start.1 = (bf16[2,1280,256]{2,1,0:T(8,128)(2,1)}, bf16[2,1280,256]{2,1,0:T(8,128)(2,1)S(1)}, u32[]{:S(2)}, u32[]{:S(2)}) collective-permute-start(bf16[2,1280,256]{2,1,0:T(8,128)(2,1)} %pad_maximum_fusion), channel_id=1, source_target_pairs={{2,0},{3,1},{4,2},{5,3},{6,4},{7,5},{8,6},{9,7},{10,8},{11,9},{12,... | collective-permute-start | bytes 3932168 | tf_op jit(solution)/shard_map/ppermute | solution.py:18
  9.2 54.3 %collective-permute-start = (bf16[2,1280,256]{2,1,0:T(8,128)(2,1)}, bf16[2,1280,256]{2,1,0:T(8,128)(2,1)}, u32[]{:S(2)}, u32[]{:S(2)}) collective-permute-start(bf16[2,1280,256]{2,1,0:T(8,128)(2,1)} %pad_maximum_fusion), channel_id=1, source_target_pairs={{14,0},{15,1},{0,2},{1,3},{2,4},{3,5},{4,6},{5,7},{6,8},{7,9},{8,1... | collective-permute-start | bytes 3932168 | tf_op jit(solution)/shard_map/ppermute | solution.py:18
  9.2 59.2 %collective-permute-start.3 = (bf16[2,1280,256]{2,1,0:T(8,128)(2,1)}, bf16[2,1280,256]{2,1,0:T(8,128)(2,1)}, u32[]{:S(2)}, u32[]{:S(2)}) collective-permute-start(bf16[2,1280,256]{2,1,0:T(8,128)(2,1)} %pad_maximum_fusion), channel_id=1, source_target_pairs={{0,1},{1,0},{2,3},{3,2},{4,5},{5,4},{6,7},{7,6},{8,9},{9,8},{10,11... | collective-permute-start | bytes 3932168 | tf_op jit(solution)/shard_map/ppermute | solution.py:23
  9.3 57.7 %collective-permute-start.4 = (bf16[2,128,256]{2,1,0:T(8,128)(2,1)S(1)}, bf16[2,128,256]{2,1,0:T(8,128)(2,1)S(1)}, u32[]{:S(2)}, u32[]{:S(2)}) collective-permute-start(bf16[2,128,256]{2,1,0:T(8,128)(2,1)S(1)} %pad_maximum_fusion.1), channel_id=1, source_target_pairs={{8,0},{9,1},{10,2},{11,3},{12,4},{13,5},{14,6},{15,7},{0,8},{1,9},... | collective-permute-start | bytes 393224 | tf_op jit(solution)/shard_map/ppermute | solution.py:18
  9.6 56.6 %copy-start.6 = (s32[20,15]{0,1:T(8,128)S(1)}, s32[20,15]{0,1:T(8,128)}, u32[]{:S(2)}) copy-start(s32[20,15]{0,1:T(8,128)} %param.14) | copy-start | bytes 3604
  63.3 1.5 copy-start.4
  64.7 4.3 %collective-permute-start.2 = (bf16[2,1280,256]{2,1,0:T(8,128)(2,1)}, bf16[2,1280,256]{2,1,0:T(8,128)(2,1)}, u32[]{:S(2)}, u32[]{:S(2)}) collective-permute-start(bf16[2,1280,256]{2,1,0:T(8,128)(2,1)} %broadcast_select_fusion.2), channel_id=1, source_target_pairs={{0,1},{1,0},{2,3},{3,2},{4,5},{5,4},{6,7},{7,6},{8,9},{9,8},{10,11... | collective-permute-start | bytes 3932168 | tf_op jit(solution)/shard_map/ppermute | solution.py:23
  70.9 1.1 copy-start.3
  72.1 1.3 copy-start.5
  73.5 2.9 %copy-start = (bf16[5,2,1408,256]{3,2,1,0:T(8,128)(2,1)}, bf16[5,2,1408,256]{3,2,1,0:T(8,128)(2,1)S(1)}, u32[]{:S(2)}) copy-start(bf16[5,2,1408,256]{3,2,1,0:T(8,128)(2,1)S(1)} %bitcast_dynamic-update-slice_fusion.kv) | copy-start | bytes 21626884
  76.4 60.9 %copy-start.7 = (f32[2]{0:T(128)S(1)}, f32[2]{0:T(128)}, u32[]{:S(2)}) copy-start(f32[2]{0:T(128)} %constant.114.clone) | copy-start | bytes 28
  144.0 3.1 %collective-permute-start.6 = (bf16[2,1280,256]{2,1,0:T(8,128)(2,1)S(1)}, bf16[2,1280,256]{2,1,0:T(8,128)(2,1)S(1)}, u32[]{:S(2)}, u32[]{:S(2)}) collective-permute-start(bf16[2,1280,256]{2,1,0:T(8,128)(2,1)S(1)} %get-tuple-element.38), channel_id=1, source_target_pairs={{0,1},{1,0},{2,3},{3,2},{4,5},{5,4},{6,7},{7,6},{8,9},{9,8},{10,11... | collective-permute-start | bytes 3932168 | tf_op jit(solution)/shard_map/ppermute | solution.py:23
  144.4 42.7 %collective-permute-start.5 = (bf16[2,1280,256]{2,1,0:T(8,128)(2,1)S(1)}, bf16[2,1280,256]{2,1,0:T(8,128)(2,1)S(1)}, u32[]{:S(2)}, u32[]{:S(2)}) collective-permute-start(bf16[2,1280,256]{2,1,0:T(8,128)(2,1)S(1)} %get-tuple-element.37), channel_id=1, source_target_pairs={{0,1},{1,0},{2,3},{3,2},{4,5},{5,4},{6,7},{7,6},{8,9},{9,8},{10,11... | collective-permute-start | bytes 3932168 | tf_op jit(solution)/shard_map/ppermute | solution.py:23
  147.8 59.2 %collective-permute-start.7 = (bf16[2,1280,256]{2,1,0:T(8,128)(2,1)S(1)}, bf16[2,1280,256]{2,1,0:T(8,128)(2,1)S(1)}, u32[]{:S(2)}, u32[]{:S(2)}) collective-permute-start(bf16[2,1280,256]{2,1,0:T(8,128)(2,1)S(1)} %get-tuple-element.31), channel_id=1, source_target_pairs={{14,0},{15,1},{0,2},{1,3},{2,4},{3,5},{4,6},{5,7},{6,8},{7,9},{8,1... | collective-permute-start | bytes 3932168 | tf_op jit(solution)/shard_map/ppermute | solution.py:18
  150.3 58.9 %collective-permute-start.8 = (bf16[2,1280,256]{2,1,0:T(8,128)(2,1)S(1)}, bf16[2,1280,256]{2,1,0:T(8,128)(2,1)S(1)}, u32[]{:S(2)}, u32[]{:S(2)}) collective-permute-start(bf16[2,1280,256]{2,1,0:T(8,128)(2,1)S(1)} %get-tuple-element.32), channel_id=1, source_target_pairs={{2,0},{3,1},{4,2},{5,3},{6,4},{7,5},{8,6},{9,7},{10,8},{11,9},{12,... | collective-permute-start | bytes 3932168 | tf_op jit(solution)/shard_map/ppermute | solution.py:18
  152.6 34.5 %collective-permute-start.9 = (bf16[2,128,256]{2,1,0:T(8,128)(2,1)S(1)}, bf16[2,128,256]{2,1,0:T(8,128)(2,1)S(1)}, u32[]{:S(2)}, u32[]{:S(2)}) collective-permute-start(bf16[2,128,256]{2,1,0:T(8,128)(2,1)S(1)} %pad_maximum_fusion.2), channel_id=1, source_target_pairs={{8,0},{9,1},{10,2},{11,3},{12,4},{13,5},{14,6},{15,7},{0,8},{1,9},... | collective-permute-start | bytes 393224 | tf_op jit(solution)/shard_map/ppermute | solution.py:18

commit v2 on v1

--- a/solution.py
+++ b/solution.py
@@ -11,16 +11,6 @@
 HEADS = 8
 REACH = 2
 SLOTS = 2 * REACH + 1
-
-
-def shifted(block, distance):
-    n = lax.axis_size("patch")
-    return lax.ppermute(block, "patch", [((i - distance) % n, i) for i in range(n)])
-
-
-def swapped(block):
-    n = lax.axis_size("patch")
-    return lax.ppermute(block, "patch", [(i, i ^ 1) for i in range(n)])
 
 
 def block_diagonal(rows):
@@ -82,14 +72,235 @@
     grad_queries[rows, :] = (folded[:block] + folded[block:]) * scale
 
 
-def kernel(block, bias, queries, grad_out, kv, grad_queries, totals, probs, grads):
-    totals[...] = jnp.zeros_like(totals)
-
-    def step(band, carry):
-        attend_band(band, block, bias, queries, grad_out, kv, totals, grad_queries, probs, grads)
+def kernel(
+    block,
+    bias,
+    queries,
+    grad_out,
+    key_rows,
+    value_rows,
+    grad_queries,
+    grad_keys,
+    grad_values,
+    kv,
+    totals,
+    probs,
+    grads,
+    far_out,
+    far_in,
+    near_out,
+    near_in,
+    merged_out,
+    merged_in,
+    plain_out,
+    plain_in,
+    pole_out,
+    pole_in,
+    send,
+    recv,
+    pole_send,
+    pole_recv,
+):
+    tokens, features = queries.shape
+    bands = tokens // block
+    scale = (features // HEADS) ** (-0.5)
+    n = lax.axis_size("patch")
+    me = lax.axis_index("patch")
+    odd = lax.rem(me, 2)
+    partner = me + 1 - 2 * odd
+    after = lax.rem(me + REACH, n)
+    before = lax.rem(me + n - REACH, n)
+    across = lax.rem(me + n // 2, n)
+    last = 2 * REACH
+
+    def at(band):
+        return pl.ds(pl.multiple_of(band * block, block), block)
+
+    def padded(band):
+        return at(band + 1)
+
+    def remote(source, target, stream, band, device):
+        return pltpu.make_async_remote_copy(
+            src_ref=source,
+            dst_ref=target,
+            send_sem=send.at[stream, band],
+            recv_sem=recv.at[stream, band],
+            device_id={"patch": device},
+            device_id_type=pl.DeviceIdType.MESH,
+        )
+
+    def keys_after(band):
+        own = kv.at[REACH, :, padded(band), :]
+        return remote(own, kv.at[0, :, padded(band), :], 0, band, after)
+
+    def keys_before(band):
+        own = kv.at[REACH, :, padded(band), :]
+        return remote(own, kv.at[last, :, padded(band), :], 1, band, before)
+
+    def keys_near(band):
+        own = kv.at[REACH, :, padded(band), :]
+        return remote(own, kv.at[1 + 2 * odd, :, padded(band), :], 2, band, partner)
+
+    def keys_far(band):
+        fetched = kv.at[last - last * odd, :, padded(band), :]
+        return remote(fetched, kv.at[3 - 2 * odd, :, padded(band), :], 3, band, partner)
+
+    def sums_far(band):
+        return remote(far_out.at[:, at(band), :], far_in.at[:, at(band), :], 4, band, partner)
+
+    def sums_near(band):
+        return remote(near_out.at[:, at(band), :], near_in.at[:, at(band), :], 5, band, partner)
+
+    def sums_merged(band):
+        device = lax.rem(me + n + REACH - 2 * REACH * odd, n)
+        return remote(merged_out.at[:, at(band), :], merged_in.at[:, at(band), :], 6, band, device)
+
+    def sums_plain(band):
+        device = lax.rem(me + n - REACH + 2 * REACH * odd, n)
+        return remote(plain_out.at[:, at(band), :], plain_in.at[:, at(band), :], 7, band, device)
+
+    def pole_copy(source, target, which):
+        return pltpu.make_async_remote_copy(
+            src_ref=source,
+            dst_ref=target,
+            send_sem=pole_send.at[which],
+            recv_sem=pole_recv.at[which],
+            device_id={"patch": across},
+            device_id_type=pl.DeviceIdType.MESH,
+        )
+
+    def pole_keys(which):
+        edge = 0 if which == 0 else bands - 1
+        beyond = -1 if which == 0 else bands
+        return pole_copy(kv.at[REACH, :, padded(edge), :], kv.at[REACH, :, padded(beyond), :], which)
+
+    def pole_sums(which):
+        return pole_copy(pole_out.at[which], pole_in.at[which], 2 + which)
+
+    def each_band(body):
+        def step(band, carry):
+            body(band)
+            return carry
+
+        lax.fori_loop(0, bands, step, 0)
+
+    def scaled(part, value):
+        return value * jnp.float32(scale) if part == 0 else value
+
+    barrier = pltpu.get_barrier_semaphore()
+    for device in (after, before, partner, across):
+        pl.semaphore_signal(
+            barrier, inc=1, device_id={"patch": device}, device_id_type=pl.DeviceIdType.MESH
+        )
+    kv[REACH, 0, block : block + tokens, :] = key_rows[...]
+    kv[REACH, 1, block : block + tokens, :] = value_rows[...]
+    pl.semaphore_wait(barrier, 4)
+
+    pole_keys(0).start()
+
+    @each_band
+    def _(band):
+        keys_after(band).start()
+        keys_before(band).start()
+        keys_near(band).start()
+
+    pole_keys(1).start()
+
+    blank = jnp.zeros((2, block, features), kv.dtype)
+    for slot in range(SLOTS):
+        if slot != REACH:
+            kv[slot, :, :block, :] = blank
+            kv[slot, :, block + tokens :, :] = blank
+    for slot in range(SLOTS):
+        for part in range(2):
+            totals[slot, part] = jnp.zeros(totals.shape[2:], jnp.float32)
+
+    def step(t, carry):
+        @pl.when(t < bands)
+        def _():
+            keys_after(t).wait_recv()
+            keys_before(t).wait_recv()
+            keys_far(t).start()
+
+        @pl.when((t >= 1) & (t <= bands))
+        def _():
+            keys_near(t - 1).wait_recv()
+            keys_far(t - 1).wait_recv()
+
+        @pl.when(t == 2)
+        def _():
+            pole_keys(0).wait_recv()
+
+        @pl.when(t == bands + 1)
+        def _():
+            pole_keys(1).wait_recv()
+
+        @pl.when((t >= 2) & (t <= bands + 1))
+        def _():
+            attend_band(
+                t - 2, block, bias, queries, grad_out, kv, totals, grad_queries, probs, grads
+            )
+
+        @pl.when((t >= 3) & (t <= bands + 2))
+        def _():
+            band = t - 3
+            for part in range(2):
+                far = scaled(part, totals[1 + 2 * odd, part, padded(band), :])
+                far_out[part, at(band), :] = far.astype(jnp.bfloat16)
+                near = scaled(part, totals[3 - 2 * odd, part, padded(band), :])
+                near_out[part, at(band), :] = near.astype(jnp.bfloat16)
+            sums_far(band).start()
+            sums_near(band).start()
+
+        @pl.when(t >= 4)
+        def _():
+            band = t - 4
+            sums_far(band).wait_recv()
+            for part in range(2):
+                merged = scaled(part, totals[last - last * odd, part, padded(band), :])
+                merged = merged + far_in[part, at(band), :].astype(jnp.float32)
+                merged_out[part, at(band), :] = merged.astype(jnp.bfloat16)
+                plain = scaled(part, totals[last * odd, part, padded(band), :])
+                plain_out[part, at(band), :] = plain.astype(jnp.bfloat16)
+            sums_merged(band).start()
+            sums_plain(band).start()
+
         return carry
 
-    lax.fori_loop(0, queries.shape[0] // block, step, 0)
+    lax.fori_loop(0, bands + 4, step, 0)
+
+    for which, beyond in ((0, -1), (1, bands)):
+        for part in range(2):
+            value = scaled(part, totals[REACH, part, padded(beyond), :])
+            pole_out[which, part] = value.astype(jnp.bfloat16)
+        pole_sums(which).start()
+
+    @each_band
+    def _(band):
+        sums_near(band).wait_recv()
+        sums_merged(band).wait_recv()
+        sums_plain(band).wait_recv()
+        for part, result in ((0, grad_keys), (1, grad_values)):
+            value = scaled(part, totals[REACH, part, padded(band), :])
+            for arrived in (near_in, merged_in, plain_in):
+                value = value + arrived[part, at(band), :].astype(jnp.float32)
+            result[at(band), :] = value
+
+    for which, edge in ((0, 0), (1, bands - 1)):
+        pole_sums(which).wait_recv()
+        for part, result in ((0, grad_keys), (1, grad_values)):
+            result[at(edge), :] += pole_in[which, part].astype(jnp.float32)
+
+    @each_band
+    def _(band):
+        for copy in (keys_after, keys_before, keys_near, keys_far):
+            copy(band).wait_send()
+        for copy in (sums_far, sums_near, sums_merged, sums_plain):
+            copy(band).wait_send()
+
+    for which in range(2):
+        pole_keys(which).wait_send()
+        pole_sums(which).wait_send()
 
 
 def bias_of(window_blocks):
@@ -111,60 +322,34 @@
     tokens, features = queries.shape
     bands = window_blocks.shape[0]
     block = tokens // bands
-    half_turn = lax.axis_size("patch") // 2
-    even = lax.axis_index("patch") % 2 == 0
-    bias = bias_of(window_blocks)
-    own = jnp.stack([key_rows, value_rows])
-    after = shifted(own, -2)
-    before = shifted(own, 2)
-    near = swapped(own)
-    far = swapped(jnp.where(even, after, before))
-    poles = shifted(jnp.concatenate([own[:, :block], own[:, tokens - block :]], axis=1), half_turn)
-    pad = lambda x: jnp.pad(x, ((0, 0), (block, block), (0, 0)))
-    kv = jnp.stack(
-        [
-            pad(before),
-            pad(jnp.where(even, far, near)),
-            jnp.concatenate([poles[:, :block], own, poles[:, block:]], axis=1),
-            pad(jnp.where(even, near, far)),
-            pad(after),
-        ]
-    )
     vmem = pl.BlockSpec(memory_space=pltpu.VMEM)
-    grad_rows, totals = pl.pallas_call(
+    result = jax.ShapeDtypeStruct((tokens, features), jnp.float32)
+    padded = tokens + 2 * block
+    wide = pltpu.VMEM((SLOTS * 3 * block, HEADS * block), jnp.float32)
+    travelling = pltpu.VMEM((2, tokens, features), jnp.bfloat16)
+    pole = pltpu.VMEM((2, 2, block, features), jnp.bfloat16)
+    return pl.pallas_call(
         functools.partial(kernel, block),
-        out_shape=(
-            jax.ShapeDtypeStruct((tokens, features), jnp.float32),
-            jax.ShapeDtypeStruct(kv.shape, jnp.float32),
+        out_shape=(result, result, result),
+        in_specs=[pl.BlockSpec(memory_space=pltpu.SMEM), vmem, vmem, vmem, vmem],
+        out_specs=(vmem, vmem, vmem),
+        scratch_shapes=[
+            pltpu.VMEM((SLOTS, 2, padded, features), jnp.bfloat16),
+            pltpu.VMEM((SLOTS, 2, padded, features), jnp.float32),
+            wide,
+            wide,
+            *([travelling] * 8),
+            pole,
+            pole,
+            pltpu.SemaphoreType.DMA((8, bands)),
+            pltpu.SemaphoreType.DMA((8, bands)),
+            pltpu.SemaphoreType.DMA((4,)),
+            pltpu.SemaphoreType.DMA((4,)),
+        ],
+        compiler_params=pltpu.CompilerParams(
+            collective_id=0, has_side_effects=True, vmem_limit_bytes=60 * 2**20
         ),
-        in_specs=[pl.BlockSpec(memory_space=pltpu.SMEM), vmem, vmem, vmem],
-        out_specs=(vmem, vmem),
-        scratch_shapes=[
-            pltpu.VMEM((SLOTS * 3 * block, HEADS * block), jnp.float32),
-            pltpu.VMEM((SLOTS * 3 * block, HEADS * block), jnp.float32),
-        ],
-        compiler_params=pltpu.CompilerParams(vmem_limit_bytes=56 * 2**20),
-    )(bias, queries, grad_out, kv)
-    scale = jnp.array([(features // HEADS) ** (-0.5), 1.0], jnp.float32)[:, None, None]
-    totals = totals * scale
-    inner = totals[:, :, block : block + tokens]
-    low = inner.astype(jnp.bfloat16)
-    far = swapped(jnp.where(even, low[1], low[3])).astype(jnp.float32)
-    zero = jnp.zeros_like(far)
-    to_after = (inner[4] + jnp.where(even, far, zero)).astype(jnp.bfloat16)
-    to_before = (inner[0] + jnp.where(even, zero, far)).astype(jnp.bfloat16)
-    near = swapped(jnp.where(even, low[3], low[1])).astype(jnp.float32)
-    pole_parts = jnp.concatenate([totals[2, :, :block], totals[2, :, block + tokens :]], axis=1)
-    pole_back = shifted(pole_parts.astype(jnp.bfloat16), half_turn).astype(jnp.float32)
-    owned = (
-        inner[2]
-        + near
-        + shifted(to_after, 2).astype(jnp.float32)
-        + shifted(to_before, -2).astype(jnp.float32)
-    )
-    owned = owned.at[:, :block].add(pole_back[:, :block])
-    owned = owned.at[:, tokens - block :].add(pole_back[:, block:])
-    return grad_rows, owned[0], owned[1]
+    )(bias_of(window_blocks), queries, grad_out, key_rows, value_rows)
 
 
 def solution(mesh):

time: 212 us -> 133 us (0.63)
  waiting for transfers between devices: 113 us -> 0 us
  Pallas kernels: 60.9 us -> 125 us
  starting transfers between devices: 13 us -> 0 us
  other arithmetic: 14 us -> 1.07 us
  local copies, waits for them, and re-layouts: 9.17 us -> 6.11 us
    ppermute x10 -> x0, waiting for transfers between devices: 113 us -> none  [the longest x6 110 us: shifted(): lax.ppermute(block, 'patch', [((i - distance) % n, i) for i in range(n)])]
    pallas_call x1, Pallas kernels: 60.9 us -> 125 us  [local(): pl.pallas_call(functools.partial(kernel, block), out_shape=(result, resul...]
    ppermute x10 -> x0, starting transfers between devices: 13 us -> none  [the longest x6 11.1 us: shifted(): lax.ppermute(block, 'patch', [((i - distance) % n, i) for i in range(n)])]
    another operation x3 -> x0, other arithmetic: 8.98 us -> none
    select_n x3 -> x0, other arithmetic: 3.28 us -> none  [the longest x1 1.88 us: local(): jnp.where(even, near, far)]
    unnamed x19 -> x7, local copies, waits for them, and re-layouts: 6.7 us -> 5.41 us
  transfers between devices with their start and end apart: 10 -> 0, of which waited for: 7 -> 0; matrix products, arithmetic and copies ran while one was open for 2% -> 0% of each run, Pallas kernels for 0% -> 0%
where the time goes in v2:
time: 133 us
  Pallas kernels  125 us (94%)
  local copies, waits for them, and re-layouts  6.11 us (5%)
    pallas_call x1, Pallas kernels, local(): pl.pallas_call(functools.partial(kernel, block), out_shape=(result, resul...  125 us
    unnamed x7, local copies, waits for them, and re-layouts  5.41 us

profile of v2, /device:TPU:0, one launch (start us, length us, event | category | flops | bytes accessed | tf_op | source)
XLA Modules:
  0.0 133.1 jit_solution(5202772279548656528)
XLA Ops:
  0.7 0.1 compare_and_fusion
  0.8 0.1 iota_add_fusion
  0.8 0.1 broadcast_select_fusion.1
  0.9 0.1 add_select_fusion
  1.0 0.7 compare_reduce_fusion
  1.8 0.7 copy.11.bias
  2.4 125.3 %shard_map.76 = (f32[1280,256]{1,0:T(8,128)}, f32[1280,256]{1,0:T(8,128)}, f32[1280,256]{1,0:T(8,128)}) custom-call(f32[20,15]{1,0:T(8,128)} %copy.11.bias, bf16[1280,256]{1,0:T(8,128)(2,1)} %queries.1, bf16[1280,256]{1,0:T(8,128)(2,1)} %grad_out.1, bf16[1280,256]{1,0:T(8,128)(2,1)} %key_rows.1, bf16[1280,256]{1,0:T(8,128)(2,1)} %value_rows.1), custom_call_target="tpu_custom_call" | custom-call | tf_op jit(solution)/shard_map/pallas_call | solution.py:331
  127.7 0.0 copy-start.1
  127.7 2.6 %copy.15 = f32[1280,256]{1,0:T(8,128)} copy(f32[1280,256]{1,0:T(8,128)} %get-tuple-element.6) | data formatting | bytes 2621440
  130.3 0.0 copy-done.1
  130.3 0.0 copy-start
  130.3 1.1 copy.16
  131.3 0.7 copy-done
  132.1 1.1 copy.17
  (6 shorter events, 0.0 us)
Async XLA Ops:
  127.7 2.6 %copy-start.1 = (f32[1280,256]{1,0:T(8,128)S(1)}, f32[1280,256]{1,0:T(8,128)}, u32[]{:S(2)}) copy-start(f32[1280,256]{1,0:T(8,128)} %get-tuple-element.7) | copy-start | bytes 3932164
  130.3 1.8 %copy-start = (f32[1280,256]{1,0:T(8,128)S(1)}, f32[1280,256]{1,0:T(8,128)}, u32[]{:S(2)}) copy-start(f32[1280,256]{1,0:T(8,128)} %get-tuple-element.8) | copy-start | bytes 3932164

commit v3 on v2

--- a/solution.py
+++ b/solution.py
@@ -86,14 +86,12 @@
     totals,
     probs,
     grads,
-    far_out,
     far_in,
-    near_out,
     near_in,
-    merged_out,
-    merged_in,
-    plain_out,
-    plain_in,
+    relay_out,
+    relay_in,
+    mate_out,
+    mate_in,
     pole_out,
     pole_in,
     send,
@@ -107,11 +105,15 @@
     n = lax.axis_size("patch")
     me = lax.axis_index("patch")
     odd = lax.rem(me, 2)
+    side = lax.rem(me // 2, 2)
     partner = me + 1 - 2 * odd
-    after = lax.rem(me + REACH, n)
-    before = lax.rem(me + n - REACH, n)
+    mate = me + 2 - 4 * side
+    ahead = lax.rem(me + 4, n)
+    behind = lax.rem(me + n - 4, n)
     across = lax.rem(me + n // 2, n)
     last = 2 * REACH
+    mate_slot = last - last * side
+    relay_slot = last * side
 
     def at(band):
         return pl.ds(pl.multiple_of(band * block, block), block)
@@ -129,13 +131,14 @@
             device_id_type=pl.DeviceIdType.MESH,
         )
 
-    def keys_after(band):
+    def keys_mate(band):
         own = kv.at[REACH, :, padded(band), :]
-        return remote(own, kv.at[0, :, padded(band), :], 0, band, after)
-
-    def keys_before(band):
-        own = kv.at[REACH, :, padded(band), :]
-        return remote(own, kv.at[last, :, padded(band), :], 1, band, before)
+        return remote(own, kv.at[relay_slot, :, padded(band), :], 0, band, mate)
+
+    def keys_relay(band):
+        device = lax.rem(me + n + 4 - 8 * side, n)
+        fetched = kv.at[mate_slot, :, padded(band), :]
+        return remote(fetched, kv.at[relay_slot, :, padded(band), :], 1, band, device)
 
     def keys_near(band):
         own = kv.at[REACH, :, padded(band), :]
@@ -146,18 +149,19 @@
         return remote(fetched, kv.at[3 - 2 * odd, :, padded(band), :], 3, band, partner)
 
     def sums_far(band):
-        return remote(far_out.at[:, at(band), :], far_in.at[:, at(band), :], 4, band, partner)
+        source = totals.at[1 + 2 * odd, :, padded(band), :]
+        return remote(source, far_in.at[:, at(band), :], 4, band, partner)
 
     def sums_near(band):
-        return remote(near_out.at[:, at(band), :], near_in.at[:, at(band), :], 5, band, partner)
-
-    def sums_merged(band):
-        device = lax.rem(me + n + REACH - 2 * REACH * odd, n)
-        return remote(merged_out.at[:, at(band), :], merged_in.at[:, at(band), :], 6, band, device)
-
-    def sums_plain(band):
-        device = lax.rem(me + n - REACH + 2 * REACH * odd, n)
-        return remote(plain_out.at[:, at(band), :], plain_in.at[:, at(band), :], 7, band, device)
+        source = totals.at[3 - 2 * odd, :, padded(band), :]
+        return remote(source, near_in.at[:, at(band), :], 5, band, partner)
+
+    def sums_relay(band):
+        device = lax.rem(me + n - 4 + 8 * side, n)
+        return remote(relay_out.at[:, at(band), :], relay_in.at[:, at(band), :], 6, band, device)
+
+    def sums_mate(band):
+        return remote(mate_out.at[:, at(band), :], mate_in.at[:, at(band), :], 7, band, mate)
 
     def pole_copy(source, target, which):
         return pltpu.make_async_remote_copy(
@@ -188,20 +192,19 @@
         return value * jnp.float32(scale) if part == 0 else value
 
     barrier = pltpu.get_barrier_semaphore()
-    for device in (after, before, partner, across):
+    for device in (mate, partner, ahead, behind, across):
         pl.semaphore_signal(
             barrier, inc=1, device_id={"patch": device}, device_id_type=pl.DeviceIdType.MESH
         )
     kv[REACH, 0, block : block + tokens, :] = key_rows[...]
     kv[REACH, 1, block : block + tokens, :] = value_rows[...]
-    pl.semaphore_wait(barrier, 4)
+    pl.semaphore_wait(barrier, 5)
 
     pole_keys(0).start()
 
     @each_band
     def _(band):
-        keys_after(band).start()
-        keys_before(band).start()
+        keys_mate(band).start()
         keys_near(band).start()
 
     pole_keys(1).start()
@@ -215,76 +218,87 @@
         for part in range(2):
             totals[slot, part] = jnp.zeros(totals.shape[2:], jnp.float32)
 
-    def step(t, carry):
-        @pl.when(t < bands)
-        def _():
-            keys_after(t).wait_recv()
-            keys_before(t).wait_recv()
-            keys_far(t).start()
-
-        @pl.when((t >= 1) & (t <= bands))
-        def _():
-            keys_near(t - 1).wait_recv()
-            keys_far(t - 1).wait_recv()
-
-        @pl.when(t == 2)
-        def _():
-            pole_keys(0).wait_recv()
-
-        @pl.when(t == bands + 1)
-        def _():
-            pole_keys(1).wait_recv()
-
-        @pl.when((t >= 2) & (t <= bands + 1))
-        def _():
-            attend_band(
-                t - 2, block, bias, queries, grad_out, kv, totals, grad_queries, probs, grads
-            )
-
-        @pl.when((t >= 3) & (t <= bands + 2))
-        def _():
-            band = t - 3
-            for part in range(2):
-                far = scaled(part, totals[1 + 2 * odd, part, padded(band), :])
-                far_out[part, at(band), :] = far.astype(jnp.bfloat16)
-                near = scaled(part, totals[3 - 2 * odd, part, padded(band), :])
-                near_out[part, at(band), :] = near.astype(jnp.bfloat16)
-            sums_far(band).start()
-            sums_near(band).start()
-
-        @pl.when(t >= 4)
-        def _():
-            band = t - 4
-            sums_far(band).wait_recv()
-            for part in range(2):
-                merged = scaled(part, totals[last - last * odd, part, padded(band), :])
-                merged = merged + far_in[part, at(band), :].astype(jnp.float32)
-                merged_out[part, at(band), :] = merged.astype(jnp.bfloat16)
-                plain = scaled(part, totals[last * odd, part, padded(band), :])
-                plain_out[part, at(band), :] = plain.astype(jnp.bfloat16)
-            sums_merged(band).start()
-            sums_plain(band).start()
-
-        return carry
-
-    lax.fori_loop(0, bands + 4, step, 0)
-
-    for which, beyond in ((0, -1), (1, bands)):
+    def send_pole_sums(which, beyond):
         for part in range(2):
             value = scaled(part, totals[REACH, part, padded(beyond), :])
             pole_out[which, part] = value.astype(jnp.bfloat16)
         pole_sums(which).start()
 
+    def step(t, carry):
+        @pl.when(t < bands)
+        def _():
+            keys_mate(t).wait_recv()
+            keys_relay(t).start()
+
+        @pl.when((t >= 1) & (t <= bands))
+        def _():
+            keys_near(t - 1).wait_recv()
+            keys_relay(t - 1).wait_recv()
+            keys_far(t - 1).start()
+
+        @pl.when((t >= 2) & (t <= bands + 1))
+        def _():
+            keys_far(t - 2).wait_recv()
+
+        @pl.when(t == 3)
+        def _():
+            pole_keys(0).wait_recv()
+
+        @pl.when(t == bands + 2)
+        def _():
+            pole_keys(1).wait_recv()
+
+        @pl.when((t >= 3) & (t <= bands + 2))
+        def _():
+            attend_band(
+                t - 3, block, bias, queries, grad_out, kv, totals, grad_queries, probs, grads
+            )
+
+        @pl.when(t == 4)
+        def _():
+            send_pole_sums(0, -1)
+
+        @pl.when(t == bands + 3)
+        def _():
+            send_pole_sums(1, bands)
+
+        @pl.when((t >= 4) & (t <= bands + 3))
+        def _():
+            sums_far(t - 4).start()
+            sums_near(t - 4).start()
+
+        @pl.when((t >= 5) & (t <= bands + 4))
+        def _():
+            band = t - 5
+            sums_far(band).wait_recv()
+            for part in range(2):
+                totals[last - last * odd, part, padded(band), :] += far_in[part, at(band), :]
+                value = scaled(part, totals[relay_slot, part, padded(band), :])
+                relay_out[part, at(band), :] = value.astype(jnp.bfloat16)
+            sums_relay(band).start()
+
+        @pl.when(t >= 6)
+        def _():
+            band = t - 6
+            sums_relay(band).wait_recv()
+            for part in range(2):
+                value = scaled(part, totals[mate_slot, part, padded(band), :])
+                value = value + relay_in[part, at(band), :].astype(jnp.float32)
+                mate_out[part, at(band), :] = value.astype(jnp.bfloat16)
+            sums_mate(band).start()
+
+        return carry
+
+    lax.fori_loop(0, bands + 6, step, 0)
+
     @each_band
     def _(band):
         sums_near(band).wait_recv()
-        sums_merged(band).wait_recv()
-        sums_plain(band).wait_recv()
+        sums_mate(band).wait_recv()
         for part, result in ((0, grad_keys), (1, grad_values)):
-            value = scaled(part, totals[REACH, part, padded(band), :])
-            for arrived in (near_in, merged_in, plain_in):
-                value = value + arrived[part, at(band), :].astype(jnp.float32)
-            result[at(band), :] = value
+            value = totals[REACH, part, padded(band), :] + near_in[part, at(band), :]
+            arrived = mate_in[part, at(band), :].astype(jnp.float32)
+            result[at(band), :] = scaled(part, value) + arrived
 
     for which, edge in ((0, 0), (1, bands - 1)):
         pole_sums(which).wait_recv()
@@ -293,9 +307,9 @@
 
     @each_band
     def _(band):
-        for copy in (keys_after, keys_before, keys_near, keys_far):
+        for copy in (keys_mate, keys_relay, keys_near, keys_far):
             copy(band).wait_send()
-        for copy in (sums_far, sums_near, sums_merged, sums_plain):
+        for copy in (sums_far, sums_near, sums_relay, sums_mate):
             copy(band).wait_send()
 
     for which in range(2):
@@ -326,6 +340,7 @@
     result = jax.ShapeDtypeStruct((tokens, features), jnp.float32)
     padded = tokens + 2 * block
     wide = pltpu.VMEM((SLOTS * 3 * block, HEADS * block), jnp.float32)
+    whole = pltpu.VMEM((2, tokens, features), jnp.float32)
     travelling = pltpu.VMEM((2, tokens, features), jnp.bfloat16)
     pole = pltpu.VMEM((2, 2, block, features), jnp.bfloat16)
     return pl.pallas_call(
@@ -338,7 +353,9 @@
             pltpu.VMEM((SLOTS, 2, padded, features), jnp.float32),
             wide,
             wide,
-            *([travelling] * 8),
+            whole,
+            whole,
+            *([travelling] * 4),
             pole,
             pole,
             pltpu.SemaphoreType.DMA((8, bands)),

time: 133 us -> 117 us (0.88)
  Pallas kernels: 125 us -> 109 us
    pallas_call x1, Pallas kernels: 125 us -> 109 us  [local(): pl.pallas_call(functools.partial(kernel, block), out_shape=(result, resul...]
where the time goes in v3:
time: 117 us
  Pallas kernels  109 us (93%)
  local copies, waits for them, and re-layouts  6.11 us (5%)
    pallas_call x1, Pallas kernels, local(): pl.pallas_call(functools.partial(kernel, block), out_shape=(result, resul...  109 us
    unnamed x7, local copies, waits for them, and re-layouts  5.41 us

profile of v3, /device:TPU:0, one launch (start us, length us, event | category | flops | bytes accessed | tf_op | source)
XLA Modules:
  0.0 117.2 jit_solution(229502421942277313)
XLA Ops:
  0.7 0.1 compare_and_fusion
  0.8 0.1 iota_add_fusion
  0.8 0.1 broadcast_select_fusion.1
  0.9 0.1 add_select_fusion
  1.0 0.7 compare_reduce_fusion
  1.8 0.7 copy.11.bias
  2.4 109.4 %shard_map.76 = (f32[1280,256]{1,0:T(8,128)}, f32[1280,256]{1,0:T(8,128)}, f32[1280,256]{1,0:T(8,128)}) custom-call(f32[20,15]{1,0:T(8,128)} %copy.11.bias, bf16[1280,256]{1,0:T(8,128)(2,1)} %queries.1, bf16[1280,256]{1,0:T(8,128)(2,1)} %grad_out.1, bf16[1280,256]{1,0:T(8,128)(2,1)} %key_rows.1, bf16[1280,256]{1,0:T(8,128)(2,1)} %value_rows.1), custom_call_target="tpu_custom_call" | custom-call | tf_op jit(solution)/shard_map/pallas_call | solution.py:346
  111.8 0.0 copy-start.1
  111.8 2.6 %copy.15 = f32[1280,256]{1,0:T(8,128)} copy(f32[1280,256]{1,0:T(8,128)} %get-tuple-element.6) | data formatting | bytes 2621440
  114.4 0.0 copy-done.1
  114.4 0.0 copy-start
  114.4 1.1 copy.16
  115.4 0.7 copy-done
  116.2 1.1 copy.17
  (6 shorter events, 0.0 us)
Async XLA Ops:
  111.8 2.6 %copy-start.1 = (f32[1280,256]{1,0:T(8,128)S(1)}, f32[1280,256]{1,0:T(8,128)}, u32[]{:S(2)}) copy-start(f32[1280,256]{1,0:T(8,128)} %get-tuple-element.7) | copy-start | bytes 3932164
  114.4 1.8 %copy-start = (f32[1280,256]{1,0:T(8,128)S(1)}, f32[1280,256]{1,0:T(8,128)}, u32[]{:S(2)}) copy-start(f32[1280,256]{1,0:T(8,128)} %get-tuple-element.8) | copy-start | bytes 3932164

commit v4 on v3

--- a/solution.py
+++ b/solution.py
@@ -202,12 +202,12 @@
 
     pole_keys(0).start()
 
-    @each_band
-    def _(band):
+    def send_keys(band):
         keys_mate(band).start()
         keys_near(band).start()
 
-    pole_keys(1).start()
+    for band in range(7):
+        send_keys(band)
 
     blank = jnp.zeros((2, block, features), kv.dtype)
     for slot in range(SLOTS):
@@ -225,51 +225,59 @@
         pole_sums(which).start()
 
     def step(t, carry):
+        @pl.when(t < bands - 7)
+        def _():
+            send_keys(t + 7)
+
+        @pl.when(t == bands - 7)
+        def _():
+            pole_keys(1).start()
+
         @pl.when(t < bands)
         def _():
             keys_mate(t).wait_recv()
             keys_relay(t).start()
 
-        @pl.when((t >= 1) & (t <= bands))
-        def _():
-            keys_near(t - 1).wait_recv()
-            keys_relay(t - 1).wait_recv()
-            keys_far(t - 1).start()
-
-        @pl.when((t >= 2) & (t <= bands + 1))
-        def _():
-            keys_far(t - 2).wait_recv()
-
-        @pl.when(t == 3)
+        @pl.when((t >= 3) & (t < bands + 3))
+        def _():
+            keys_near(t - 3).wait_recv()
+            keys_relay(t - 3).wait_recv()
+            keys_far(t - 3).start()
+
+        @pl.when((t >= 4) & (t < bands + 4))
+        def _():
+            keys_far(t - 4).wait_recv()
+
+        @pl.when(t == 5)
         def _():
             pole_keys(0).wait_recv()
 
-        @pl.when(t == bands + 2)
+        @pl.when(t == bands + 4)
         def _():
             pole_keys(1).wait_recv()
 
-        @pl.when((t >= 3) & (t <= bands + 2))
+        @pl.when((t >= 5) & (t < bands + 5))
         def _():
             attend_band(
-                t - 3, block, bias, queries, grad_out, kv, totals, grad_queries, probs, grads
+                t - 5, block, bias, queries, grad_out, kv, totals, grad_queries, probs, grads
             )
 
-        @pl.when(t == 4)
+        @pl.when(t == 6)
         def _():
             send_pole_sums(0, -1)
 
-        @pl.when(t == bands + 3)
+        @pl.when(t == bands + 5)
         def _():
             send_pole_sums(1, bands)
 
-        @pl.when((t >= 4) & (t <= bands + 3))
-        def _():
-            sums_far(t - 4).start()
-            sums_near(t - 4).start()
-
-        @pl.when((t >= 5) & (t <= bands + 4))
-        def _():
-            band = t - 5
+        @pl.when((t >= 6) & (t < bands + 6))
+        def _():
+            sums_far(t - 6).start()
+            sums_near(t - 6).start()
+
+        @pl.when((t >= 8) & (t < bands + 8))
+        def _():
+            band = t - 8
             sums_far(band).wait_recv()
             for part in range(2):
                 totals[last - last * odd, part, padded(band), :] += far_in[part, at(band), :]
@@ -277,9 +285,9 @@
                 relay_out[part, at(band), :] = value.astype(jnp.bfloat16)
             sums_relay(band).start()
 
-        @pl.when(t >= 6)
-        def _():
-            band = t - 6
+        @pl.when(t >= 11)
+        def _():
+            band = t - 11
             sums_relay(band).wait_recv()
             for part in range(2):
                 value = scaled(part, totals[mate_slot, part, padded(band), :])
@@ -289,7 +297,7 @@
 
         return carry
 
-    lax.fori_loop(0, bands + 6, step, 0)
+    lax.fori_loop(0, bands + 11, step, 0)
 
     @each_band
     def _(band):

time: 117 us -> 99.4 us (0.85); the launches traced: 117 us -> 98.2 us
  Pallas kernels: 109 us -> 90.3 us
    pallas_call x1, Pallas kernels: 109 us -> 90.3 us  [local(): pl.pallas_call(functools.partial(kernel, block), out_shape=(result, resul...]
where the time goes in v4:
time: 99.4 us; the launch traced here: 98.2 us
  Pallas kernels  90.3 us (91%)
  local copies, waits for them, and re-layouts  6.11 us (6%)
  other arithmetic  1.07 us (1%)
    pallas_call x1, Pallas kernels, local(): pl.pallas_call(functools.partial(kernel, block), out_shape=(result, resul...  90.3 us
    unnamed x7, local copies, waits for them, and re-layouts  5.41 us

profile of v4, /device:TPU:0, one launch (start us, length us, event | category | flops | bytes accessed | tf_op | source)
XLA Modules:
  0.0 98.2 jit_solution(16165280383238497258)
XLA Ops:
  0.7 0.1 compare_and_fusion
  0.8 0.1 iota_add_fusion
  0.8 0.1 broadcast_select_fusion.1
  0.9 0.1 add_select_fusion
  1.0 0.7 compare_reduce_fusion
  1.8 0.7 copy.11.bias
  2.4 90.3 %shard_map.76 = (f32[1280,256]{1,0:T(8,128)}, f32[1280,256]{1,0:T(8,128)}, f32[1280,256]{1,0:T(8,128)}) custom-call(f32[20,15]{1,0:T(8,128)} %copy.11.bias, bf16[1280,256]{1,0:T(8,128)(2,1)} %queries.1, bf16[1280,256]{1,0:T(8,128)(2,1)} %grad_out.1, bf16[1280,256]{1,0:T(8,128)(2,1)} %key_rows.1, bf16[1280,256]{1,0:T(8,128)(2,1)} %value_rows.1), custom_call_target="tpu_custom_call" | custom-call | tf_op jit(solution)/shard_map/pallas_call | solution.py:354
  92.7 0.0 copy-start.1
  92.7 2.6 %copy.15 = f32[1280,256]{1,0:T(8,128)} copy(f32[1280,256]{1,0:T(8,128)} %get-tuple-element.6) | data formatting | bytes 2621440
  95.3 0.0 copy-done.1
  95.3 0.0 copy-start
  95.3 1.1 %copy.16 = f32[1280,256]{1,0:T(8,128)} copy(f32[1280,256]{1,0:T(8,128)S(1)} %copy-done.1) | data formatting | bytes 2621440
  96.4 0.7 copy-done
  97.1 1.1 %copy.17 = f32[1280,256]{1,0:T(8,128)} copy(f32[1280,256]{1,0:T(8,128)S(1)} %copy-done) | data formatting | bytes 2621440
  (6 shorter events, 0.0 us)
Async XLA Ops:
  92.7 2.6 %copy-start.1 = (f32[1280,256]{1,0:T(8,128)S(1)}, f32[1280,256]{1,0:T(8,128)}, u32[]{:S(2)}) copy-start(f32[1280,256]{1,0:T(8,128)} %get-tuple-element.7) | copy-start | bytes 3932164
  95.3 1.8 %copy-start = (f32[1280,256]{1,0:T(8,128)S(1)}, f32[1280,256]{1,0:T(8,128)}, u32[]{:S(2)}) copy-start(f32[1280,256]{1,0:T(8,128)} %get-tuple-element.8) | copy-start | bytes 3932164
